TPU v7x, 32 devices: a whole 2x2x4 slice. The times are simulated.
32 devices in a mesh: grp: 2 (over y), req: 4 (over z), hid: 2 (over x), kv: 2 (over core).
Axes of the slice: x: 2, y: 2, z: 4, core: 2. Of those that a mesh axis runs over, the one named last changes fastest.
Arguments:
- residual: bfloat16 [256, 3072], P(('grp', 'req', 'hid', 'kv')), parts along dimension 0, may hold values from -6 to 6
- queries: bfloat16 [16, 16, 3072], P(('grp', 'req', 'hid'), None, 'kv'), parts along dimension 0, may hold values from -220 to 220
- tree_row_keys: bfloat16 [16, 16, 512], P(('grp', 'req', 'hid'), None, 'kv'), parts along dimension 0, may hold values from -6 to 6
- tree_row_values: bfloat16 [16, 16, 512], P(('grp', 'req', 'hid'), None, 'kv'), parts along dimension 0, may hold values from -6 to 6
- cache_keys: bfloat16 [16, 1024, 512], P(('grp', 'req', 'hid'), None, 'kv'), parts along dimension 0, may hold values from -6 to 6
- stored_values: bfloat16 [16, 1024, 512], P(('grp', 'req', 'hid'), None, 'kv'), parts along dimension 0, may hold values from -6 to 6
- cache_lengths: int32 [16], P(('grp', 'req', 'hid')), parts along dimension 0, may hold values from 128 to 1024, as said below
- tree_sizes: int32 [16], P(('grp', 'req', 'hid')), parts along dimension 0, may hold values from 1 to 16, as said below
- tree_mask: int32 [16, 16, 16], P(('grp', 'req', 'hid')), parts along dimension 0, may hold values from 0 to 1, as said below
- routes: int32 [256, 2], P(('grp', 'req', 'hid', 'kv')), parts along dimension 0, may hold values from 0 to 3, all different within a row; in each aligned block of 8 rows (0 to 7, 8 to 15, ...) at most 5 rows name the same one
- norm_gain: bfloat16 [3072], replicated, may hold values from 0.099609375 to 1.8984375
- router: bfloat16 [3072, 4], replicated, may hold values from -0.109375 to 0.109375
- gate_weight: bfloat16 [3072, 32768], P('kv', ('req', 'hid')), may hold values from -0.109375 to 0.109375
- up_weight: bfloat16 [3072, 32768], P('kv', ('req', 'hid')), may hold values from -0.109375 to 0.109375
- down_weight: bfloat16 [32768, 3072], P(('req', 'hid'), 'kv'), may hold values from -0.0625 to 0.0625
Outputs:
- expert_mix: bfloat16 [256, 3072], P(('grp', 'req', 'hid', 'kv')), parts along dimension 0
- hidden_state: bfloat16 [256, 3072], P(('grp', 'req', 'hid', 'kv')), parts along dimension 0
There are 2 independent parts, one for each index of `grp`. A program takes and returns all parts, laid end to end along the dimension named above; an argument that names none is the same for every part. Nothing has to cross between parts.
Inputs may be any that keep to these rules, and one draw needn't show every extreme that they name: `cache_lengths`: some request has exactly 1024 live slots. `tree_sizes`: some request has exactly 16 live rows. tree_mask[b, t, u] is 1 exactly when u is t or an ancestor of t in request b's tree; every row's parent has a lower index; row 0 is the root. `routes`: the two experts of a row differ; within each aligned block of 8 rows (the rows of one device), no expert is named by more than 5 rows.
All inputs are finite; a program needn't handle non-finite values.
Results may differ from a plain program's by a relative error of at most 0.009.
Values may be sent and summed in bfloat16 or wider, within the bound.
A program may use at most 256 MiB of HBM per device.

v0:
```python
import math

import jax
import jax.numpy as jnp
from jax import lax
from jax.sharding import PartitionSpec as P

HEAD_SIZE = 128
EXPERTS = 4


def attend_request(
    query_rows,
    tree_key_rows,
    tree_value_rows,
    cache_key_rows,
    cache_value_rows,
    length,
    tree_size,
    mask_r,
):
    tree_len = query_rows.shape[0]
    cache_len = cache_key_rows.shape[0]
    kv_heads = cache_key_rows.shape[1] // HEAD_SIZE
    query_count = query_rows.shape[1] // HEAD_SIZE
    heads_per_group = query_count // kv_heads
    query_head_count = query_rows.reshape(tree_len, kv_heads, heads_per_group, HEAD_SIZE)
    cache_key_block = cache_key_rows.reshape(cache_len, kv_heads, HEAD_SIZE)
    cache_value_block = cache_value_rows.reshape(cache_len, kv_heads, HEAD_SIZE)
    tree_key_block = tree_key_rows.reshape(tree_len, kv_heads, HEAD_SIZE)
    tree_value_block = tree_value_rows.reshape(tree_len, kv_heads, HEAD_SIZE)
    scale = 1.0 / math.sqrt(HEAD_SIZE)
    cache_scores = (
        jnp.einsum(
            "tgqd,cgd->gqtc", query_head_count, cache_key_block, preferred_element_type=jnp.float32
        )
        * scale
    )
    tree_scores = (
        jnp.einsum(
            "tgqd,ugd->gqtu", query_head_count, tree_key_block, preferred_element_type=jnp.float32
        )
        * scale
    )
    cache_live = jnp.arange(cache_len, dtype=jnp.int32) < length
    tree_live = (mask_r > 0) & (jnp.arange(tree_len, dtype=jnp.int32)[None, :] < tree_size)
    cache_scores = jnp.where(cache_live[None, None, None, :], cache_scores, -1e30)
    tree_scores = jnp.where(tree_live[None, None], tree_scores, -1e30)
    highest = jnp.maximum(cache_scores.max(-1), tree_scores.max(-1))
    cache_exp = jnp.exp(cache_scores - highest[..., None])
    tree_exp = jnp.exp(tree_scores - highest[..., None])
    summed = cache_exp.sum(-1) + tree_exp.sum(-1)
    cache_prob = (cache_exp / summed[..., None]).astype(jnp.bfloat16)
    tree_prob = (tree_exp / summed[..., None]).astype(jnp.bfloat16)
    output = jnp.einsum(
        "gqtc,cgd->tgqd", cache_prob, cache_value_block, preferred_element_type=jnp.float32
    )
    output = output + jnp.einsum(
        "gqtu,ugd->tgqd", tree_prob, tree_value_block, preferred_element_type=jnp.float32
    )
    return output.reshape(tree_len, query_count * HEAD_SIZE).astype(jnp.bfloat16)


def place_rows(route_block, capacity):
    flat_routes = route_block.reshape(-1)
    onehot = (flat_routes[:, None] == jnp.arange(EXPERTS, dtype=jnp.int32)[None, :]).astype(
        jnp.int32
    )
    before = jnp.cumsum(onehot, axis=0) - onehot
    position = jnp.sum(before * onehot, axis=1)
    return flat_routes * capacity + position


def local(
    residual,
    queries,
    tree_row_keys,
    tree_row_values,
    cache_keys,
    stored_values,
    cache_lengths,
    tree_sizes,
    tree_mask,
    routes,
    norm_gain,
    router,
    gate_weight,
    up_weight,
    down_weight,
):
    attended = jax.vmap(attend_request)(
        queries,
        tree_row_keys,
        tree_row_values,
        cache_keys,
        stored_values,
        cache_lengths,
        tree_sizes,
        tree_mask,
    )
    head_rows = attended.reshape(-1, attended.shape[-1])
    own_rows = lax.all_to_all(head_rows, "kv", split_axis=0, concat_axis=1, tiled=True)
    stream = residual.astype(jnp.float32) + own_rows.astype(jnp.float32)
    normed = (
        stream
        * lax.rsqrt(jnp.mean(stream * stream, axis=-1, keepdims=True) + 1e-05)
        * norm_gain.astype(jnp.float32)
    ).astype(jnp.bfloat16)
    row_count = normed.shape[0]
    width = normed.shape[1]
    capacity = row_count * 2 // EXPERTS + max(1, row_count // 8)
    targets = place_rows(routes, capacity)
    picker = (jnp.arange(EXPERTS * capacity, dtype=jnp.int32)[:, None] == targets[None, :]).astype(
        jnp.bfloat16
    )
    blocks = jnp.dot(
        picker, jnp.repeat(normed, 2, axis=0), preferred_element_type=jnp.float32
    ).astype(jnp.bfloat16)
    gate_full, up_full, down_full = (
        lax.all_gather(gate_weight, "kv", axis=0, tiled=True),
        lax.all_gather(up_weight, "kv", axis=0, tiled=True),
        lax.all_gather(down_weight, "kv", axis=1, tiled=True),
    )
    req_count = lax.axis_size("req")
    group_size = req_count // EXPERTS
    outgoing = jnp.repeat(blocks.reshape(EXPERTS, capacity, width), group_size, axis=0)
    arrived = lax.all_to_all(outgoing, "req", split_axis=0, concat_axis=0, tiled=True)
    inputs = lax.all_gather(arrived.reshape(-1, width), "hid", axis=0, tiled=True)
    gate = jnp.dot(inputs, gate_full, preferred_element_type=jnp.float32)
    up_part = jnp.dot(inputs, up_full, preferred_element_type=jnp.float32)
    hidden = (jax.nn.silu(gate) * up_part).astype(jnp.bfloat16)
    partial_out = jnp.dot(hidden, down_full, preferred_element_type=jnp.float32)
    reduced = lax.psum_scatter(
        partial_out.astype(jnp.bfloat16), "hid", scatter_dimension=0, tiled=True
    ).astype(jnp.float32)
    returned = lax.all_to_all(
        reduced.reshape(req_count, capacity, width).astype(jnp.bfloat16),
        "req",
        split_axis=0,
        concat_axis=0,
        tiled=True,
    ).astype(jnp.float32)
    expert_sums = (
        returned.reshape(EXPERTS, group_size, capacity, width)
        .sum(axis=1)
        .reshape(EXPERTS * capacity, width)
    )
    picked = expert_sums[targets].reshape(row_count, 2, width)
    logits = jnp.dot(normed, router, preferred_element_type=jnp.float32)
    chosen = jnp.take_along_axis(logits, routes, axis=1)
    gates = jax.nn.softmax(chosen, axis=-1)
    mixture = jnp.sum(gates[:, :, None] * picked, axis=1)
    return (mixture.astype(jnp.bfloat16), (stream + mixture).astype(jnp.bfloat16))


def solution(mesh):
    placed = (
        P(("grp", "req", "hid", "kv"), None),
        P(("grp", "req", "hid"), None, "kv"),
        P(("grp", "req", "hid"), None, "kv"),
        P(("grp", "req", "hid"), None, "kv"),
        P(("grp", "req", "hid"), None, "kv"),
        P(("grp", "req", "hid"), None, "kv"),
        P(("grp", "req", "hid")),
        P(("grp", "req", "hid")),
        P(("grp", "req", "hid"), None, None),
        P(("grp", "req", "hid", "kv"), None),
        P(),
        P(),
        P("kv", ("req", "hid")),
        P("kv", ("req", "hid")),
        P(("req", "hid"), "kv"),
    )
    return jax.shard_map(
        local,
        mesh=mesh,
        in_specs=placed,
        out_specs=(P(("grp", "req", "hid", "kv"), None), P(("grp", "req", "hid", "kv"), None)),
        check_vma=False,
    )
```

profile of v0, /device:TPU:0, one launch (start us, length us, event | category | flops | bytes accessed | tf_op | source)
XLA Modules:
  0.0 194.4 jit_solution(1409843317273995439)
XLA Ops:
  7.3 0.7 all-gather.5.cloned.1.call-update
  8.1 0.7 all-gather.7.cloned.1.call-update
  8.8 0.7 all-gather.9.cloned.1.call-update
  11.3 0.2 fusion.35
  11.6 0.4 fusion.34
  12.0 0.3 fusion.9
  12.3 0.4 fusion.15
  12.7 0.2 fusion.8
  12.9 0.7 convert_element_type.75
  13.6 3.3 %all-to-all-start = ((bf16[2,8,1536]{2,1,0:T(8,128)(2,1)}), bf16[2,8,1536]{2,1,0:T(8,128)(2,1)S(1)}, u32[]{:S(2)}, u32[]{:S(2)}) async-start(bf16[2,8,1536]{2,1,0:T(8,128)(2,1)} %convert_element_type.75), calls=%async_computation | async-start | bytes 98304 | tf_op jit(solution)/shard_map/all_to_all | solution.py:102
  17.0 1.3 all-to-all-done
  19.2 0.7 reshape_broadcast_in_dim_reshape.3
  20.0 6.3 %all-to-all-start.1 = ((bf16[4,5,3072]{2,1,0:T(8,128)(2,1)}), bf16[4,5,3072]{2,1,0:T(8,128)(2,1)S(1)}, u32[]{:S(2)}, u32[]{:S(2)}) async-start(bf16[4,5,3072]{2,1,0:T(8,128)(2,1)} %reshape_broadcast_in_dim_reshape.3), calls=%async_computation.1 | async-start | bytes 393216 | tf_op jit(solution)/shard_map/all_to_all | solution.py:127
  26.7 0.7 gather_fusion.1
  28.0 6.2 %all-to-all-done.1 = bf16[4,5,3072]{2,1,0:T(8,128)(2,1)S(1)} async-done(((bf16[4,5,3072]{2,1,0:T(8,128)(2,1)}), bf16[4,5,3072]{2,1,0:T(8,128)(2,1)S(1)}, u32[]{:S(2)}, u32[]{:S(2)}) %all-to-all-start.1) | async-done | bytes 122912 | tf_op jit(solution)/shard_map/all_to_all | solution.py:127
  34.2 5.8 %all-gather = bf16[2,20,3072]{2,1,0:T(8,128)(2,1)S(1)} all-gather(bf16[1,20,3072]{2,1,0:T(8,128)(2,1)S(1)} %reshape.251), channel_id=1, replica_groups=mesh['grp'=2,'req'=4,'hid'=2,'kv'=2] {'hid'}, dimensions={0}, use_global_device_ids=true | all-gather | bytes 368640 | tf_op jit(solution)/shard_map/all_gather | solution.py:128
  40.1 12.6 %all-gather.5.cloned.1.call-done = bf16[3072,4096]{1,0:T(8,128)(2,1)} async-done(((bf16[1536,4096]{1,0:T(8,128)(2,1)}), bf16[3072,4096]{1,0:T(8,128)(2,1)}) %all-gather.5.cloned.1.call-update) | async-done | bytes 25165840 | tf_op jit(solution)/shard_map/all_gather | solution.py:120
  52.7 10.4 %fusion.37 = f32[40,4096]{1,0:T(8,128)S(1)} fusion(bf16[40,3072]{1,0:T(8,128)(2,1)S(1)} %reshape.252, bf16[3072,4096]{1,0:T(8,128)(2,1)} %all-gather.5.cloned.1.call-done), kind=kOutput, calls=%fused_computation.71 | convolution fusion | flops 1006632960 | bytes 26066944 | tf_op jit(solution)/shard_map/dot_general | solution.py:129
  63.1 32.6 %all-gather.7.cloned.1.call-done = bf16[3072,4096]{1,0:T(8,128)(2,1)} async-done(((bf16[1536,4096]{1,0:T(8,128)(2,1)}), bf16[3072,4096]{1,0:T(8,128)(2,1)}) %all-gather.7.cloned.1.call-update) | async-done | bytes 25165840 | tf_op jit(solution)/shard_map/all_gather | solution.py:121
  95.7 45.3 %all-gather.9.cloned.1.call-done = bf16[4096,3072]{1,0:T(8,128)(2,1)} async-done(((bf16[4096,1536]{1,0:T(8,128)(2,1)}), bf16[4096,3072]{1,0:T(8,128)(2,1)}) %all-gather.9.cloned.1.call-update) | async-done | bytes 25165840 | tf_op jit(solution)/shard_map/all_gather | solution.py:122
  141.0 20.0 %convolution_convert_fusion = bf16[40,3072]{1,0:T(8,128)(2,1)S(1)} fusion(bf16[4096,3072]{1,0:T(8,128)(2,1)} %all-gather.9.cloned.1.call-done, bf16[40,3072]{1,0:T(8,128)(2,1)S(1)} %reshape.252, bf16[3072,4096]{1,0:T(8,128)(2,1)} %all-gather.7.cloned.1.call-done, f32[40,4096]{1,0:T(8,128)S(1)} %fusion.37), kind=kOutput, calls=%fused_computation.4 | convolution fusion | flops 2014371840 | bytes 51478528 | tf_op jit(solution)/shard_map/dot_general | solution.py:132
  161.0 9.2 %fusion = bf16[24,3072]{1,0:T(8,128)(2,1)S(1)} fusion(bf16[40,3072]{1,0:T(8,128)(2,1)S(1)} %convolution_convert_fusion), kind=kCustom, calls=%all-reduce-scatter | all-reduce-scatter fusion | flops 147457 | bytes 393728
  170.2 2.2 %collective-permute-start = (bf16[4,3072]{1,0:T(4,128)(2,1)S(1)}, bf16[4,3072]{1,0:T(4,128)(2,1)S(1)}, u32[]{:S(2)}, u32[]{:S(2)}) collective-permute-start(bf16[4,3072]{1,0:T(4,128)(2,1)S(1)} %slice.4), channel_id=1, source_target_pairs={{0,2},{1,3},{4,6},{5,7},{8,10},{9,11},{12,14},{13,15},{16,18},{17,... | collective-permute-start | bytes 73736
  172.4 0.6 dynamic-slice.4
  173.6 0.2 collective-permute-done
  173.9 0.4 concatenate.3
  174.3 0.7 convert_element_type.85
  175.0 4.9 %all-to-all-start.2 = ((bf16[4,5,3072]{2,1,0:T(8,128)(2,1)}), bf16[4,5,3072]{2,1,0:T(8,128)(2,1)S(1)}, u32[]{:S(2)}, u32[]{:S(2)}) async-start(bf16[4,5,3072]{2,1,0:T(8,128)(2,1)} %convert_element_type.85), calls=%async_computation.2 | async-start | bytes 393216 | tf_op jit(solution)/shard_map/all_to_all | solution.py:136
  179.9 6.2 %all-to-all-done.2 = bf16[4,5,3072]{2,1,0:T(8,128)(2,1)S(1)} async-done(((bf16[4,5,3072]{2,1,0:T(8,128)(2,1)}), bf16[4,5,3072]{2,1,0:T(8,128)(2,1)S(1)}, u32[]{:S(2)}, u32[]{:S(2)}) %all-to-all-start.2) | async-done | bytes 122912 | tf_op jit(solution)/shard_map/all_to_all | solution.py:136
  186.2 0.6 gather_fusion
  186.9 0.3 multiply_reduce_fusion
  187.2 0.7 add_convert_fusion
  (73 shorter events, 3.0 us)
Async XLA Ops:
  7.2 19.4 %copy-start = (bf16[3072,4]{0,1:T(4,128)(2,1)S(1)}, bf16[3072,4]{0,1:T(4,128)(2,1)}, u32[]{:S(2)}) copy-start(bf16[3072,4]{0,1:T(4,128)(2,1)} %param.26) | copy-start | bytes 73732
  7.2 2.3 %copy-start.4 = (bf16[1,16,1536]{2,1,0:T(8,128)(2,1)S(1)}, bf16[1,16,1536]{2,1,0:T(8,128)(2,1)}, u32[]{:S(2)}) copy-start(bf16[1,16,1536]{2,1,0:T(8,128)(2,1)} %param.16) | copy-start | bytes 147460
  7.2 2.4 %copy-start.1 = (bf16[1,1024,256]{2,1,0:T(8,128)(2,1)S(1)}, bf16[1,1024,256]{2,1,0:T(8,128)(2,1)}, u32[]{:S(2)}) copy-start(bf16[1,1024,256]{2,1,0:T(8,128)(2,1)} %param.19) | copy-start | bytes 1572868
  7.2 3.2 %copy-start.5 = (bf16[1,16,256]{2,1,0:T(8,128)(2,1)S(1)}, bf16[1,16,256]{2,1,0:T(8,128)(2,1)}, u32[]{:S(2)}) copy-start(bf16[1,16,256]{2,1,0:T(8,128)(2,1)} %param.17) | copy-start | bytes 24580
  7.2 3.9 %copy-start.6 = (s32[1,16,16]{2,1,0:T(8,128)S(1)}, s32[1,16,16]{2,1,0:T(8,128)}, u32[]{:S(2)}) copy-start(s32[1,16,16]{2,1,0:T(8,128)} %param.23) | copy-start | bytes 3076
  7.2 4.0 %copy-start.2 = (bf16[1,1024,256]{2,1,0:T(8,128)(2,1)S(1)}, bf16[1,1024,256]{2,1,0:T(8,128)(2,1)}, u32[]{:S(2)}) copy-start(bf16[1,1024,256]{2,1,0:T(8,128)(2,1)} %param.20) | copy-start | bytes 1572868
  7.2 4.1 %copy-start.7 = (bf16[1,16,256]{2,1,0:T(8,128)(2,1)S(1)}, bf16[1,16,256]{2,1,0:T(8,128)(2,1)}, u32[]{:S(2)}) copy-start(bf16[1,16,256]{2,1,0:T(8,128)(2,1)} %param.18) | copy-start | bytes 24580
  7.2 9.7 %copy-start.8 = (bf16[3072]{0:T(1024)(128)(2,1)S(1)}, bf16[3072]{0:T(1024)(128)(2,1)}, u32[]{:S(2)}) copy-start(bf16[3072]{0:T(1024)(128)(2,1)} %param.25) | copy-start | bytes 18436
  7.3 9.7 %copy-start.9 = (s32[8,2]{0,1:T(2,128)S(1)}, s32[8,2]{0,1:T(2,128)}, u32[]{:S(2)}) copy-start(s32[8,2]{0,1:T(2,128)} %param.24) | copy-start | bytes 196
  7.3 11.0 %copy-start.3 = (bf16[8,3072]{1,0:T(8,128)(2,1)S(1)}, bf16[8,3072]{1,0:T(8,128)(2,1)}, u32[]{:S(2)}) copy-start(bf16[8,3072]{1,0:T(8,128)(2,1)} %param.15) | copy-start | bytes 147460
  7.3 45.4 %all-gather.5.cloned.1.call-start = ((), (), s32[]{:S(2)}) async-start(), calls=%async_computation.3 | async-start | bytes 37748736 | tf_op jit(solution)/shard_map/all_gather | solution.py:120
  8.0 87.7 %all-gather.7.cloned.1.call-start = ((), (), s32[]{:S(2)}) async-start(), calls=%async_computation.4 | async-start | bytes 37748736 | tf_op jit(solution)/shard_map/all_gather | solution.py:121
  8.8 132.2 %all-gather.9.cloned.1.call-start = ((), (), s32[]{:S(2)}) async-start(), calls=%async_computation.5 | async-start | bytes 37748736 | tf_op jit(solution)/shard_map/all_gather | solution.py:122
  13.6 4.7 %all-to-all-start = ((bf16[2,8,1536]{2,1,0:T(8,128)(2,1)}), bf16[2,8,1536]{2,1,0:T(8,128)(2,1)S(1)}, u32[]{:S(2)}, u32[]{:S(2)}) async-start(bf16[2,8,1536]{2,1,0:T(8,128)(2,1)} %convert_element_type.75), calls=%async_computation | async-start | bytes 98304 | tf_op jit(solution)/shard_map/all_to_all | solution.py:102
  20.0 14.2 %all-to-all-start.1 = ((bf16[4,5,3072]{2,1,0:T(8,128)(2,1)}), bf16[4,5,3072]{2,1,0:T(8,128)(2,1)S(1)}, u32[]{:S(2)}, u32[]{:S(2)}) async-start(bf16[4,5,3072]{2,1,0:T(8,128)(2,1)} %reshape_broadcast_in_dim_reshape.3), calls=%async_computation.1 | async-start | bytes 393216 | tf_op jit(solution)/shard_map/all_to_all | solution.py:127
  63.1 109.3 %copy-start.10 = (u32[32]{0:T(128)S(1)}, u32[32]{0:T(128)}, u32[]{:S(2)}) copy-start(u32[32]{0:T(128)} %constant.70) | copy-start | bytes 388
  170.2 3.7 %collective-permute-start = (bf16[4,3072]{1,0:T(4,128)(2,1)S(1)}, bf16[4,3072]{1,0:T(4,128)(2,1)S(1)}, u32[]{:S(2)}, u32[]{:S(2)}) collective-permute-start(bf16[4,3072]{1,0:T(4,128)(2,1)S(1)} %slice.4), channel_id=1, source_target_pairs={{0,2},{1,3},{4,6},{5,7},{8,10},{9,11},{12,14},{13,15},{16,18},{17,... | collective-permute-start | bytes 73736
  175.0 11.1 %all-to-all-start.2 = ((bf16[4,5,3072]{2,1,0:T(8,128)(2,1)}), bf16[4,5,3072]{2,1,0:T(8,128)(2,1)S(1)}, u32[]{:S(2)}, u32[]{:S(2)}) async-start(bf16[4,5,3072]{2,1,0:T(8,128)(2,1)} %convert_element_type.85), calls=%async_computation.2 | async-start | bytes 393216 | tf_op jit(solution)/shard_map/all_to_all | solution.py:136
Sparse Core Ops, SparseCore 0:
  9.7 42.9 all-gather.4
  54.2 41.4 all-gather.6
  97.3 43.6 all-gather.8
where the time goes:
time: 195 us; the launch traced here: 194 us
  waiting for transfers between devices  106 us (54%)
  matrix products  31.9 us (16%)
  starting transfers between devices  16.8 us (9%)
  between operations  16.1 us (8%)
  blocking collectives  15 us (8%)
  local copies, waits for them, and re-layouts  6.03 us (3%)
  other arithmetic  2.25 us (1%)
    all_gather x1, waiting for transfers between devices, local(): lax.all_gather(down_weight, 'kv', axis=1, tiled=True)  45.3 us
    all_gather x1, waiting for transfers between devices, local(): lax.all_gather(up_weight, 'kv', axis=0, tiled=True)  32.6 us
    dot_general x1, matrix products, local(): partial_out = jnp.dot(hidden, down_full, preferred_element_type=jnp.float32)  20 us
    all_gather x1, waiting for transfers between devices, local(): lax.all_gather(gate_weight, 'kv', axis=0, tiled=True)  12.6 us
    dot_general x1, matrix products, local(): gate = jnp.dot(inputs, gate_full, preferred_element_type=jnp.float32)  10.4 us
    unnamed x1, blocking collectives  9.16 us
    all_to_all x1, starting transfers between devices, local(): lax.all_to_all(outgoing, 'req', split_axis=0, concat_axis=0, tiled=True)  6.32 us
    all_to_all x1, waiting for transfers between devices, local(): lax.all_to_all(reduced.reshape(req_count, capacity, width).astype(jnp.bfl...  6.17 us
  transfers between devices with their start and end apart: 7, of which 7 were waited for; matrix products, arithmetic and copies ran while one was open for 9% of the time, Pallas kernels for 0%

commit v1 on v0

--- a/solution.py
+++ b/solution.py
@@ -3,6 +3,8 @@
 import jax
 import jax.numpy as jnp
 from jax import lax
+from jax.experimental import pallas as pl
+from jax.experimental.pallas import tpu as pltpu
 from jax.sharding import PartitionSpec as P
 
 HEAD_SIZE = 128
@@ -153,6 +155,360 @@
     return (mixture.astype(jnp.bfloat16), (stream + mixture).astype(jnp.bfloat16))
 
 
+WAYS = 4
+OUT_TILES = 3
+MESH = pl.DeviceIdType.MESH
+
+
+def layer_kernel(
+    len_ref, tsz_ref, res_ref, q_ref, tk_ref, tv_ref, mask_ref, routes_ref, gain_ref, router_ref,
+    ck_hbm, cv_hbm, wg_hbm, wu_hbm, wd_hbm,
+    mix_ref, hid_ref,
+    ck, cv, wg, wu, wd,
+    xs, xr, sq_s, sq_r, lg_s, lg_r, gates_ref, stream_ref, rows,
+    ps, pr, hidden, acc_ref, own_ref, half_s, half_r, summed, back, mixf, hidf, fin_s, fin_r,
+    kv_sem, wg_sem, wu_sem, wd_sem, tiny_s, tiny_r, row_zs, row_xs, row_r,
+    ps_s, ps_r, h_s, h_r, half_ss, half_rs, back_s, back_r,
+):
+    req, hid, kv = lax.axis_index("req"), lax.axis_index("hid"), lax.axis_index("kv")
+    n_req = rows.shape[0] // 2
+    t_rows, half = rows.shape[1], rows.shape[2]
+    piece = wg.shape[2]
+    tile = wd.shape[2]
+    o_rows = res_ref.shape[0]
+    okv, ohid = 1 - kv, 1 - hid
+    bf, f32 = jnp.bfloat16, jnp.float32
+    peer_kv, peer_hid = {"kv": okv}, {"hid": ohid}
+
+    def remote(src, dst, ss, rs, dev):
+        return pltpu.make_async_remote_copy(
+            src_ref=src, dst_ref=dst, send_sem=ss, recv_sem=rs, device_id=dev, device_id_type=MESH
+        )
+
+    copy_k = pltpu.make_async_copy(ck_hbm.at[0], ck, kv_sem.at[0])
+    copy_v = pltpu.make_async_copy(cv_hbm.at[0], cv, kv_sem.at[1])
+    copy_k.start()
+    copy_v.start()
+
+    def weight_copy(which, c):
+        hbm, ref, sem = ((wg_hbm, wg, wg_sem), (wu_hbm, wu, wu_sem))[which]
+        return pltpu.make_async_copy(
+            hbm.at[:, pl.ds(pl.multiple_of(c * piece, piece), piece)], ref.at[c], sem.at[c]
+        )
+
+    def down_copy(n):
+        return pltpu.make_async_copy(wd_hbm.at[:, pl.ds(n * tile, tile)], wd.at[n], wd_sem.at[n])
+
+    for base in (okv, kv):
+        for c in range(WAYS):
+            weight_copy(0, base * WAYS + c).start()
+            weight_copy(1, base * WAYS + c).start()
+    for n in range(OUT_TILES):
+        down_copy(n).start()
+
+    barrier = pltpu.get_barrier_semaphore()
+    others = [lax.rem(req + d, n_req) for d in range(1, n_req)]
+    for dev in [peer_kv, peer_hid] + [{"req": z} for z in others]:
+        pl.semaphore_signal(barrier, inc=1, device_id=dev, device_id_type=MESH)
+    pl.semaphore_wait(barrier, 2 + len(others))
+
+    lane = lax.broadcasted_iota(jnp.int32, (o_rows, 128), 1)
+    routes = routes_ref[...].astype(f32)
+    route_lanes = jnp.where(lane == 0, routes[:, 0:1], jnp.where(lane == 1, routes[:, 1:2], 0.0))
+    xs[:, :half] = res_ref[:, pl.ds(pl.multiple_of(okv * half, half), half)].astype(f32)
+    xs[:, half:] = route_lanes
+    swap = remote(xs, xr.at[kv], tiny_s.at[0], tiny_r.at[0], peer_kv)
+    swap.start()
+    xr[kv, :, :half] = res_ref[:, pl.ds(pl.multiple_of(kv * half, half), half)].astype(f32)
+    xr[kv, :, half:] = route_lanes
+
+    scale = 1.0 / math.sqrt(HEAD_SIZE)
+    groups = ck.shape[1] // HEAD_SIZE
+    per = half // HEAD_SIZE // groups
+    length, tsz = len_ref[0], tsz_ref[0]
+    mask = mask_ref[0]
+    mask = jnp.concatenate([mask] * per, axis=0)
+    tree_live = (mask > 0) & (lax.broadcasted_iota(jnp.int32, mask.shape, 1) < tsz)
+    slots = ck.shape[0]
+    live = lax.broadcasted_iota(jnp.int32, (1, slots), 1) < length
+    nt = (((1,), (1,)), ((), ()))
+    copy_k.wait()
+    heads = []
+    scores = []
+    for g in range(groups):
+        cols = slice(g * HEAD_SIZE, (g + 1) * HEAD_SIZE)
+        q = jnp.concatenate(
+            [q_ref[0, :, (g * per + j) * HEAD_SIZE : (g * per + j + 1) * HEAD_SIZE] for j in range(per)],
+            axis=0,
+        )
+        s = lax.dot_general(q, ck[:, cols], nt, preferred_element_type=f32) * scale
+        t = lax.dot_general(q, tk_ref[0, :, cols], nt, preferred_element_type=f32) * scale
+        scores.append((jnp.where(live, s, -1e30), jnp.where(tree_live, t, -1e30)))
+    copy_v.wait()
+    for g in range(groups):
+        cols = slice(g * HEAD_SIZE, (g + 1) * HEAD_SIZE)
+        s, t = scores[g]
+        top = jnp.maximum(s.max(-1, keepdims=True), t.max(-1, keepdims=True))
+        s, t = jnp.exp(s - top), jnp.exp(t - top)
+        inv = 1.0 / (s.sum(-1, keepdims=True) + t.sum(-1, keepdims=True))
+        o = jnp.dot((s * inv).astype(bf), cv[:, cols], preferred_element_type=f32)
+        o = o + jnp.dot((t * inv).astype(bf), tv_ref[0, :, cols], preferred_element_type=f32)
+        o = o.astype(bf).astype(f32)
+        heads += [o[j * t_rows : (j + 1) * t_rows] for j in range(per)]
+    attn = jnp.concatenate(heads, axis=1)
+
+    remote(xs, xr.at[okv], tiny_s.at[0], tiny_r.at[0], peer_kv).wait_recv()
+    both = xr[...].reshape(t_rows, half + 128)
+    stream = both[:, :half] + attn
+    stream_ref[...] = stream
+    sq_s[...] = jnp.broadcast_to(jnp.sum(stream * stream, axis=-1, keepdims=True), sq_s.shape)
+    swap_sq = remote(sq_s, sq_r, tiny_s.at[1], tiny_r.at[1], peer_kv)
+    swap_sq.start()
+    gained = gain_ref[:, pl.ds(pl.multiple_of(kv * half, half), half)].astype(f32)
+    swap_sq.wait_recv()
+    mean = (sq_s[:, 0:1] + sq_r[:, 0:1]) * (1.0 / (2 * half))
+    normed = (stream * lax.rsqrt(mean + 1e-05) * gained).astype(bf)
+
+    me = hid * n_req + req
+    rows[me] = normed
+    sends = []
+    for d, z in enumerate(others):
+        sends.append(remote(rows.at[me], rows.at[me], row_zs.at[d], row_r.at[me], {"req": z}))
+    sends.append(remote(rows.at[me], rows.at[me], row_xs.at[0], row_r.at[me], peer_hid))
+    for copy in sends:
+        copy.start()
+
+    normed = normed.astype(f32)
+    router = router_ref[:, pl.ds(pl.multiple_of(kv * half, half), half)].astype(f32)
+    lanes = lax.broadcasted_iota(jnp.int32, (t_rows, 128), 1)
+    part = jnp.zeros((t_rows, 128), f32)
+    for e in range(EXPERTS):
+        one = jnp.sum(normed * router[e : e + 1, :], axis=-1, keepdims=True)
+        part = jnp.where(lanes == e, one, part)
+    lg_s[...] = part
+    swap_lg = remote(lg_s, lg_r, tiny_s.at[2], tiny_r.at[2], peer_kv)
+    swap_lg.start()
+
+    def wait_rows(slot):
+        remote(rows.at[slot], rows.at[slot], row_xs.at[0], row_r.at[slot], peer_hid).wait_recv()
+
+    for d, z in enumerate(others):
+        slot = hid * n_req + z
+        wait_rows(slot)
+        copy = remote(rows.at[slot], rows.at[slot], row_xs.at[d + 1], row_r.at[slot], peer_hid)
+        copy.start()
+        sends.append(copy)
+
+    swap_lg.wait_recv()
+    logits = lg_s[...] + lg_r[...]
+    lane_f = lanes.astype(f32)
+    first, second = both[:, half : half + 1], both[:, half + 1 : half + 2]
+    is_first, is_second = lane_f == first, lane_f == second
+    a = jnp.sum(jnp.where(is_first, logits, 0.0), axis=-1, keepdims=True)
+    b = jnp.sum(jnp.where(is_second, logits, 0.0), axis=-1, keepdims=True)
+    ab = jnp.maximum(a, b)
+    ea, eb = jnp.exp(a - ab), jnp.exp(b - ab)
+    gates_ref[...] = jnp.where(is_first, ea / (ea + eb), jnp.where(is_second, eb / (ea + eb), 0.0))
+
+    for z in range(n_req):
+        wait_rows(ohid * n_req + lax.rem(req + z, n_req))
+
+    count = 2 * n_req * t_rows
+
+    def both_dots(c):
+        weight_copy(0, c).wait()
+        weight_copy(1, c).wait()
+        x = rows[...].reshape(count, half)
+        return (
+            jnp.dot(x, wg[c], preferred_element_type=f32),
+            jnp.dot(x, wu[c], preferred_element_type=f32),
+        )
+
+    def pair_copy(c):
+        return remote(ps.at[c], pr.at[c], ps_s.at[c], ps_r.at[c], peer_kv)
+
+    def hidden_copy(which, c):
+        view = hidden.at[which, :, pl.ds(pl.multiple_of(c * piece, piece), piece)]
+        return remote(view, view, h_s.at[c], h_r.at[c], peer_kv)
+
+    def partner_step(c, _):
+        gate, up = both_dots(okv * WAYS + c)
+        ps[c, 0] = gate.astype(bf)
+        ps[c, 1] = up.astype(bf)
+        pair_copy(c).start()
+        return 0
+
+    lax.fori_loop(0, WAYS, partner_step, 0)
+
+    def own_step(c, _):
+        gate, up = both_dots(kv * WAYS + c)
+        pair_copy(c).wait_recv()
+        gate = gate + pr[c, 0].astype(f32)
+        up = up + pr[c, 1].astype(f32)
+        value = (gate / (1.0 + jnp.exp(-gate)) * up).astype(bf)
+        hidden[kv, :, pl.ds(pl.multiple_of(c * piece, piece), piece)] = value
+        hidden_copy(kv, c).start()
+        return 0
+
+    lax.fori_loop(0, WAYS, own_step, 0)
+
+    span = WAYS * piece
+
+    def down_dot(which, n):
+        return jnp.dot(
+            hidden[which],
+            wd[n, pl.ds(pl.multiple_of(which * span, span), span), :],
+            preferred_element_type=f32,
+        )
+
+    def half_copy(n):
+        return remote(half_s.at[n], half_r.at[n], half_ss.at[n], half_rs.at[n], peer_hid)
+
+    def back_copy(n, d, z):
+        return remote(
+            summed.at[n, z], back.at[n, req], back_s.at[n, d], back_r.at[n, req], {"req": z}
+        )
+
+    def forward(n):
+        half_copy(n).wait_recv()
+        total = (own_ref[n] + half_r[n].astype(f32)).astype(bf)
+        summed[n] = total.reshape(n_req, t_rows, tile)
+        for d, z in enumerate(others):
+            back_copy(n, d, z).start()
+        back[n, req] = summed[n, req]
+
+    def down_step(n, _):
+        down_copy(n).wait()
+        acc_ref[...] = down_dot(kv, n).reshape(acc_ref.shape)
+
+        @pl.when(n == 0)
+        def _():
+            for c in range(WAYS):
+                hidden_copy(okv, c).wait_recv()
+
+        acc_ref[...] += down_dot(okv, n).reshape(acc_ref.shape)
+        half_s[n] = acc_ref[ohid].astype(bf)
+        half_copy(n).start()
+        own_ref[n] = acc_ref[hid]
+
+        @pl.when(n > 0)
+        def _():
+            forward(n - 1)
+
+        return 0
+
+    lax.fori_loop(0, OUT_TILES, down_step, 0)
+    forward(OUT_TILES - 1)
+
+    gates = gates_ref[...]
+    for n in range(OUT_TILES):
+        for z in others:
+            remote(
+                summed.at[n, z], back.at[n, z], back_s.at[n, 0], back_r.at[n, z], {"req": z}
+            ).wait_recv()
+        mix = jnp.zeros((t_rows, tile), f32)
+        for e in range(EXPERTS):
+            mix = mix + gates[:, e : e + 1] * back[n, e].astype(f32)
+        cols = slice(n * tile, (n + 1) * tile)
+        mixf[:, :, cols] = mix.reshape(2, o_rows, tile)
+        hidf[:, :, cols] = (stream_ref[:, cols] + mix).reshape(2, o_rows, tile)
+
+    fin_s[...] = jnp.concatenate([mixf[okv], hidf[okv]], axis=0).astype(bf)
+    last = remote(fin_s, fin_r, tiny_s.at[3], tiny_r.at[3], peer_kv)
+    last.start()
+    mine = pl.ds(pl.multiple_of(kv * half, half), half)
+    mix_ref[:, mine] = mixf[kv].astype(bf)
+    hid_ref[:, mine] = hidf[kv].astype(bf)
+    last.wait_recv()
+    got = fin_r[...].astype(f32)
+    theirs = pl.ds(pl.multiple_of(okv * half, half), half)
+    mix_ref[:, theirs] = got[:o_rows].astype(bf)
+    hid_ref[:, theirs] = got[o_rows:].astype(bf)
+
+    for copy in [swap, swap_sq, swap_lg, last] + sends:
+        copy.wait_send()
+    for c in range(WAYS):
+        pair_copy(c).wait_send()
+        hidden_copy(kv, c).wait_send()
+    for n in range(OUT_TILES):
+        half_copy(n).wait_send()
+        for d, z in enumerate(others):
+            back_copy(n, d, z).wait_send()
+
+
+def local_kernel(
+    residual, queries, tree_row_keys, tree_row_values, cache_keys, stored_values, cache_lengths,
+    tree_sizes, tree_mask, routes, norm_gain, router, gate_weight, up_weight, down_weight,
+):
+    bf, f32 = jnp.bfloat16, jnp.float32
+    n_req = lax.axis_size("req")
+    o_rows, width = residual.shape
+    half = width // 2
+    t_rows = queries.shape[1]
+    slots, kv_cols = cache_keys.shape[1:]
+    units = gate_weight.shape[1]
+    piece = units // 2 // WAYS
+    tile = half // OUT_TILES
+    count = 2 * n_req * t_rows
+    side = n_req * t_rows
+    vm = pl.BlockSpec(memory_space=pltpu.VMEM)
+    sm = pl.BlockSpec(memory_space=pltpu.SMEM)
+    hb = pl.BlockSpec(memory_space=pl.ANY)
+    dma = pltpu.SemaphoreType.DMA
+    scratch = [
+        pltpu.VMEM((slots, kv_cols), bf),
+        pltpu.VMEM((slots, kv_cols), bf),
+        pltpu.VMEM((2 * WAYS, half, piece), bf),
+        pltpu.VMEM((2 * WAYS, half, piece), bf),
+        pltpu.VMEM((OUT_TILES, units, tile), bf),
+        pltpu.VMEM((o_rows, half + 128), f32),
+        pltpu.VMEM((2, o_rows, half + 128), f32),
+        pltpu.VMEM((t_rows, 128), f32),
+        pltpu.VMEM((t_rows, 128), f32),
+        pltpu.VMEM((t_rows, 128), f32),
+        pltpu.VMEM((t_rows, 128), f32),
+        pltpu.VMEM((t_rows, 128), f32),
+        pltpu.VMEM((t_rows, half), f32),
+        pltpu.VMEM((2 * n_req, t_rows, half), bf),
+        pltpu.VMEM((WAYS, 2, count, piece), bf),
+        pltpu.VMEM((WAYS, 2, count, piece), bf),
+        pltpu.VMEM((2, count, units // 2), bf),
+        pltpu.VMEM((2, side, tile), f32),
+        pltpu.VMEM((OUT_TILES, side, tile), f32),
+        pltpu.VMEM((OUT_TILES, side, tile), bf),
+        pltpu.VMEM((OUT_TILES, side, tile), bf),
+        pltpu.VMEM((OUT_TILES, n_req, t_rows, tile), bf),
+        pltpu.VMEM((OUT_TILES, n_req, t_rows, tile), bf),
+        pltpu.VMEM((2, o_rows, half), f32),
+        pltpu.VMEM((2, o_rows, half), f32),
+        pltpu.VMEM((t_rows, half), bf),
+        pltpu.VMEM((t_rows, half), bf),
+        dma((2,)), dma((2 * WAYS,)), dma((2 * WAYS,)), dma((OUT_TILES,)),
+        dma((4,)), dma((4,)),
+        dma((n_req - 1,)), dma((n_req,)), dma((2 * n_req,)),
+        dma((WAYS,)), dma((WAYS,)), dma((WAYS,)), dma((WAYS,)),
+        dma((OUT_TILES,)), dma((OUT_TILES,)),
+        dma((OUT_TILES, n_req - 1)), dma((OUT_TILES, n_req)),
+    ]
+    return pl.pallas_call(
+        layer_kernel,
+        out_shape=(jax.ShapeDtypeStruct(residual.shape, bf),) * 2,
+        in_specs=[sm, sm] + [vm] * 8 + [hb] * 5,
+        out_specs=(vm, vm),
+        scratch_shapes=scratch,
+        compiler_params=pltpu.CompilerParams(
+            collective_id=0, has_side_effects=True, vmem_limit_bytes=58 * 1024 * 1024
+        ),
+        cost_estimate=pl.CostEstimate(
+            flops=6 * count * half * units, bytes_accessed=6 * half * units, transcendentals=0
+        ),
+    )(
+        cache_lengths, tree_sizes, residual, queries, tree_row_keys, tree_row_values, tree_mask,
+        routes, norm_gain.reshape(1, -1), router.T,
+        cache_keys, stored_values, gate_weight, up_weight, down_weight,
+    )
+
+
 def solution(mesh):
     placed = (
         P(("grp", "req", "hid", "kv"), None),
@@ -171,8 +527,9 @@
         P("kv", ("req", "hid")),
         P(("req", "hid"), "kv"),
     )
+    one_shard_per_expert = mesh.shape["req"] == EXPERTS and mesh.shape["hid"] == 2
     return jax.shard_map(
-        local,
+        local_kernel if one_shard_per_expert and mesh.shape["kv"] == 2 else local,
         mesh=mesh,
         in_specs=placed,
         out_specs=(P(("grp", "req", "hid", "kv"), None), P(("grp", "req", "hid", "kv"), None)),

time: 195 us -> 55.6 us (0.29)
  waiting for transfers between devices: 106 us -> 0 us
  Pallas kernels: 0 us -> 47.9 us
  matrix products: 31.9 us -> 0 us
  starting transfers between devices: 16.8 us -> 0 us
  blocking collectives: 15 us -> 0 us
  between operations: 16.1 us -> 1.93 us
  other arithmetic: 2.25 us -> 0 us
    all_gather x3 -> x0, waiting for transfers between devices: 90.5 us -> none  [the longest x1 45.3 us: local(): lax.all_gather(down_weight, 'kv', axis=1, tiled=True)]
    pallas_call x0 -> x1, Pallas kernels: none -> 47.9 us  [local_kernel(): pl.pallas_call(layer_kernel, out_shape=(jax.ShapeDtypeStruct(residual.sha...]
    dot_general x8 -> x0, matrix products: 31.9 us -> none  [the longest x1 20 us: local(): partial_out = jnp.dot(hidden, down_full, preferred_element_type=jnp.float32)]
    all_to_all x3 -> x0, starting transfers between devices: 14.5 us -> none  [the longest x1 6.32 us: local(): lax.all_to_all(outgoing, 'req', split_axis=0, concat_axis=0, tiled=True)]
    all_to_all x3 -> x0, waiting for transfers between devices: 13.6 us -> none  [the longest x1 6.17 us: local(): lax.all_to_all(reduced.reshape(req_count, capacity, width).astype(jnp.bfl...]
    unnamed x1 -> x0, blocking collectives: 9.16 us -> none
    all_gather x1 -> x0, blocking collectives: 5.82 us -> none  [local(): lax.all_gather(arrived.reshape(-1, width), 'hid', axis=0, tiled=True)]
    unnamed x29 -> x3, local copies, waits for them, and re-layouts: 1.26 us -> 4.19 us
  transfers between devices with their start and end apart: 7 -> 0, of which waited for: 7 -> 0; matrix products, arithmetic and copies ran while one was open for 9% -> 0% of each run, Pallas kernels for 0% -> 0%
where the time goes in v1:
time: 55.6 us; the launch traced here: 55.3 us
  Pallas kernels  47.9 us (86%)
  local copies, waits for them, and re-layouts  5.49 us (10%)
  between operations  1.93 us (3%)
    pallas_call x1, Pallas kernels, local_kernel(): pl.pallas_call(layer_kernel, out_shape=(jax.ShapeDtypeStruct(residual.sha...  47.9 us
    unnamed x3, local copies, waits for them, and re-layouts  4.19 us
    reshape x1, local copies, waits for them, and re-layouts, local_kernel(): norm_gain.reshape(1, -1)  1.3 us

profile of v1, /device:TPU:0, one launch (start us, length us, event | category | flops | bytes accessed | tf_op | source)
XLA Modules:
  0.0 55.3 jit_solution(16844170876009580507)
XLA Ops:
  1.9 1.3 %copy.17.routes_ref = s32[8,2]{1,0:T(8,128)} copy(s32[8,2]{0,1:T(2,128)} %param.24) | data formatting | bytes 128 | tf_op args[9]
  3.3 1.3 %reshape.7.gain_ref = bf16[1,3072]{1,0:T(2,128)(2,1)} reshape(bf16[3072]{0:T(1024)(128)(2,1)} %param.25) | data formatting | bytes 12288 | tf_op jit(solution)/shard_map/reshape | solution.py:507
  4.6 47.9 %shard_map.158 = (bf16[8,3072]{1,0:T(8,128)(2,1)}, bf16[8,3072]{1,0:T(8,128)(2,1)}) custom-call(s32[1]{0:T(128)S(6)} %copy.20.len_ref, s32[1]{0:T(128)S(6)} %copy.21.tsz_ref, bf16[8,3072]{1,0:T(8,128)(2,1)} %res_ref.1, bf16[1,16,1536]{2,1,0:T(8,128)(2,1)} %q_ref.1, bf16[1,16,256]{2,1,0:T(8,128)(2,1)} %tk_ref.1, bf16[1,16,256]{2,1,0:T(8,128)(2,1)} %tv_ref.1, ...), custom_call_target="tpu_custom_call" | custom-call | flops 4831838208 | bytes 37748736 | tf_op jit(solution)/shard_map/pallas_call | solution.py:493
  52.4 1.4 %copy.22 = bf16[8,3072]{1,0:T(8,128)(2,1)} copy(bf16[8,3072]{1,0:T(8,128)(2,1)} %get-tuple-element.4) | data formatting | bytes 98304
  53.9 1.4 %copy.23 = bf16[8,3072]{1,0:T(8,128)(2,1)} copy(bf16[8,3072]{1,0:T(8,128)(2,1)} %get-tuple-element.5) | data formatting | bytes 98304

commit v2 on v1

--- a/solution.py
+++ b/solution.py
@@ -155,15 +155,16 @@
     return (mixture.astype(jnp.bfloat16), (stream + mixture).astype(jnp.bfloat16))
 
 
-WAYS = 4
-OUT_TILES = 3
+WAYS = 2
+OUT_TILES = 2
 MESH = pl.DeviceIdType.MESH
+FAR = (1, 3, 2)
 
 
 def layer_kernel(
     len_ref, tsz_ref, res_ref, q_ref, tk_ref, tv_ref, mask_ref, routes_ref, gain_ref, router_ref,
     ck_hbm, cv_hbm, wg_hbm, wu_hbm, wd_hbm,
-    mix_ref, hid_ref,
+    out_ref,
     ck, cv, wg, wu, wd,
     xs, xr, sq_s, sq_r, lg_s, lg_r, gates_ref, stream_ref, rows,
     ps, pr, hidden, acc_ref, own_ref, half_s, half_r, summed, back, mixf, hidf, fin_s, fin_r,
@@ -199,28 +200,11 @@
     def down_copy(n):
         return pltpu.make_async_copy(wd_hbm.at[:, pl.ds(n * tile, tile)], wd.at[n], wd_sem.at[n])
 
-    for base in (okv, kv):
-        for c in range(WAYS):
-            weight_copy(0, base * WAYS + c).start()
-            weight_copy(1, base * WAYS + c).start()
-    for n in range(OUT_TILES):
-        down_copy(n).start()
 
     barrier = pltpu.get_barrier_semaphore()
-    others = [lax.rem(req + d, n_req) for d in range(1, n_req)]
+    others = [lax.rem(req + d, n_req) for d in FAR]
     for dev in [peer_kv, peer_hid] + [{"req": z} for z in others]:
         pl.semaphore_signal(barrier, inc=1, device_id=dev, device_id_type=MESH)
-    pl.semaphore_wait(barrier, 2 + len(others))
-
-    lane = lax.broadcasted_iota(jnp.int32, (o_rows, 128), 1)
-    routes = routes_ref[...].astype(f32)
-    route_lanes = jnp.where(lane == 0, routes[:, 0:1], jnp.where(lane == 1, routes[:, 1:2], 0.0))
-    xs[:, :half] = res_ref[:, pl.ds(pl.multiple_of(okv * half, half), half)].astype(f32)
-    xs[:, half:] = route_lanes
-    swap = remote(xs, xr.at[kv], tiny_s.at[0], tiny_r.at[0], peer_kv)
-    swap.start()
-    xr[kv, :, :half] = res_ref[:, pl.ds(pl.multiple_of(kv * half, half), half)].astype(f32)
-    xr[kv, :, half:] = route_lanes
 
     scale = 1.0 / math.sqrt(HEAD_SIZE)
     groups = ck.shape[1] // HEAD_SIZE
@@ -244,7 +228,28 @@
         s = lax.dot_general(q, ck[:, cols], nt, preferred_element_type=f32) * scale
         t = lax.dot_general(q, tk_ref[0, :, cols], nt, preferred_element_type=f32) * scale
         scores.append((jnp.where(live, s, -1e30), jnp.where(tree_live, t, -1e30)))
+    pl.semaphore_wait(barrier, 2 + len(others))
+
+    lane = lax.broadcasted_iota(jnp.int32, (o_rows, 128), 1)
+    routes = routes_ref[...].astype(f32)
+    square = (o_rows, o_rows)
+    diagonal = lax.broadcasted_iota(jnp.int32, square, 0) == lax.broadcasted_iota(jnp.int32, square, 1)
+    choice = [
+        jnp.sum(jnp.where(diagonal, routes[k : k + 1, :], 0.0), axis=1, keepdims=True) for k in range(2)
+    ]
+    route_lanes = jnp.where(lane == 0, choice[0], jnp.where(lane == 1, choice[1], 0.0))
+    xs[:, :half] = res_ref[:, pl.ds(pl.multiple_of(okv * half, half), half)].astype(f32)
+    xs[:, half:] = route_lanes
+    swap = remote(xs, xr.at[kv], tiny_s.at[0], tiny_r.at[0], peer_kv)
+    swap.start()
+    xr[kv, :, :half] = res_ref[:, pl.ds(pl.multiple_of(kv * half, half), half)].astype(f32)
+    xr[kv, :, half:] = route_lanes
+
     copy_v.wait()
+    for base in (okv, kv):
+        for c in range(WAYS):
+            weight_copy(0, base * WAYS + c).start()
+            weight_copy(1, base * WAYS + c).start()
     for g in range(groups):
         cols = slice(g * HEAD_SIZE, (g + 1) * HEAD_SIZE)
         s, t = scores[g]
@@ -264,7 +269,10 @@
     sq_s[...] = jnp.broadcast_to(jnp.sum(stream * stream, axis=-1, keepdims=True), sq_s.shape)
     swap_sq = remote(sq_s, sq_r, tiny_s.at[1], tiny_r.at[1], peer_kv)
     swap_sq.start()
-    gained = gain_ref[:, pl.ds(pl.multiple_of(kv * half, half), half)].astype(f32)
+    gain = gain_ref[...].astype(f32)
+    strips = half // 128
+    gain = jnp.where(kv == 0, gain[:strips], gain[strips:])
+    gained = jnp.concatenate([gain[j : j + 1] for j in range(strips)], axis=1)
     swap_sq.wait_recv()
     mean = (sq_s[:, 0:1] + sq_r[:, 0:1]) * (1.0 / (2 * half))
     normed = (stream * lax.rsqrt(mean + 1e-05) * gained).astype(bf)
@@ -313,6 +321,8 @@
     for z in range(n_req):
         wait_rows(ohid * n_req + lax.rem(req + z, n_req))
 
+    for n in range(OUT_TILES):
+        down_copy(n).start()
     count = 2 * n_req * t_rows
 
     def both_dots(c):
@@ -417,13 +427,10 @@
     last = remote(fin_s, fin_r, tiny_s.at[3], tiny_r.at[3], peer_kv)
     last.start()
     mine = pl.ds(pl.multiple_of(kv * half, half), half)
-    mix_ref[:, mine] = mixf[kv].astype(bf)
-    hid_ref[:, mine] = hidf[kv].astype(bf)
+    out_ref[:, mine] = jnp.concatenate([mixf[kv], hidf[kv]], axis=0).astype(bf)
     last.wait_recv()
-    got = fin_r[...].astype(f32)
     theirs = pl.ds(pl.multiple_of(okv * half, half), half)
-    mix_ref[:, theirs] = got[:o_rows].astype(bf)
-    hid_ref[:, theirs] = got[o_rows:].astype(bf)
+    out_ref[:, theirs] = fin_r[...]
 
     for copy in [swap, swap_sq, swap_lg, last] + sends:
         copy.wait_send()
@@ -490,11 +497,11 @@
         dma((OUT_TILES,)), dma((OUT_TILES,)),
         dma((OUT_TILES, n_req - 1)), dma((OUT_TILES, n_req)),
     ]
-    return pl.pallas_call(
+    both = pl.pallas_call(
         layer_kernel,
-        out_shape=(jax.ShapeDtypeStruct(residual.shape, bf),) * 2,
+        out_shape=jax.ShapeDtypeStruct((2 * o_rows, width), bf),
         in_specs=[sm, sm] + [vm] * 8 + [hb] * 5,
-        out_specs=(vm, vm),
+        out_specs=vm,
         scratch_shapes=scratch,
         compiler_params=pltpu.CompilerParams(
             collective_id=0, has_side_effects=True, vmem_limit_bytes=58 * 1024 * 1024
@@ -504,9 +511,10 @@
         ),
     )(
         cache_lengths, tree_sizes, residual, queries, tree_row_keys, tree_row_values, tree_mask,
-        routes, norm_gain.reshape(1, -1), router.T,
+        routes.T, norm_gain.reshape(-1, 128), router.T,
         cache_keys, stored_values, gate_weight, up_weight, down_weight,
     )
+    return both[:o_rows], both[o_rows:]
 
 
 def solution(mesh):

time: 55.6 us -> 40.3 us (0.72)
  Pallas kernels: 47.9 us -> 36.6 us
  local copies, waits for them, and re-layouts: 5.49 us -> 1.46 us
    pallas_call x1, Pallas kernels: 47.9 us -> 36.6 us  [local_kernel(): pl.pallas_call(layer_kernel, out_shape=jax.ShapeDtypeStruct((2 * o_rows,...]
    unnamed x3 -> x0, local copies, waits for them, and re-layouts: 4.19 us -> none
    slice x0 -> x1, local copies, waits for them, and re-layouts: none -> 1.46 us  [local_kernel(): return (both[:o_rows], both[o_rows:])]
    reshape x1 -> x0, local copies, waits for them, and re-layouts: 1.3 us -> none  [local_kernel(): norm_gain.reshape(1, -1)]
where the time goes in v2:
time: 40.3 us; the launch traced here: 40 us
  Pallas kernels  36.6 us (91%)
  between operations  1.93 us (5%)
  local copies, waits for them, and re-layouts  1.46 us (4%)
    pallas_call x1, Pallas kernels, local_kernel(): pl.pallas_call(layer_kernel, out_shape=jax.ShapeDtypeStruct((2 * o_rows,...  36.6 us
    slice x1, local copies, waits for them, and re-layouts, local_kernel(): return (both[:o_rows], both[o_rows:])  1.46 us

profile of v2, /device:TPU:0, one launch (start us, length us, event | category | flops | bytes accessed | tf_op | source)
XLA Modules:
  0.0 40.0 jit_solution(1934252727962278410)
XLA Ops:
  1.9 36.6 %shard_map.158 = bf16[16,3072]{1,0:T(8,128)(2,1)} custom-call(s32[1]{0:T(128)S(6)} %copy.17.len_ref, s32[1]{0:T(128)S(6)} %copy.18.tsz_ref, bf16[8,3072]{1,0:T(8,128)(2,1)} %res_ref.1, bf16[1,16,1536]{2,1,0:T(8,128)(2,1)} %q_ref.1, bf16[1,16,256]{2,1,0:T(8,128)(2,1)} %tk_ref.1, bf16[1,16,256]{2,1,0:T(8,128)(2,1)} %tv_ref.1, s32[1,16,16]{2,1,0:T(8,128)} %mask_ref.1, ...), custom_call_target="tpu_custom_call" | custom-call | flops 4831838208 | bytes 37748736 | tf_op jit(solution)/shard_map/pallas_call | solution.py:500
  38.6 1.5 %fusion = (bf16[8,3072]{1,0:T(8,128)(2,1)}, bf16[8,3072]{1,0:T(8,128)(2,1)}) fusion(bf16[16,3072]{1,0:T(8,128)(2,1)} %shard_map.158), kind=kLoop, calls=%fused_computation | loop fusion | bytes 196608 | tf_op jit(solution)/shard_map/slice | solution.py:517

commit v3 on v2

--- a/solution.py
+++ b/solution.py
@@ -279,10 +279,9 @@
 
     me = hid * n_req + req
     rows[me] = normed
-    sends = []
+    sends = [remote(rows.at[me], rows.at[me], row_xs.at[0], row_r.at[me], peer_hid)]
     for d, z in enumerate(others):
         sends.append(remote(rows.at[me], rows.at[me], row_zs.at[d], row_r.at[me], {"req": z}))
-    sends.append(remote(rows.at[me], rows.at[me], row_xs.at[0], row_r.at[me], peer_hid))
     for copy in sends:
         copy.start()
 

time: 40.3 us -> 40.3 us (level)
  no operation moved by 1% of the time
where the time goes in v3:
time: 40.3 us; the launch traced here: 40 us
  Pallas kernels  36.6 us (91%)
  between operations  1.93 us (5%)
  local copies, waits for them, and re-layouts  1.46 us (4%)
    pallas_call x1, Pallas kernels, local_kernel(): pl.pallas_call(layer_kernel, out_shape=jax.ShapeDtypeStruct((2 * o_rows,...  36.6 us
    slice x1, local copies, waits for them, and re-layouts, local_kernel(): return (both[:o_rows], both[o_rows:])  1.46 us

profile of v3, /device:TPU:0, one launch (start us, length us, event | category | flops | bytes accessed | tf_op | source)
XLA Modules:
  0.0 40.0 jit_solution(9985699067171553359)
XLA Ops:
  1.9 36.6 %shard_map.158 = bf16[16,3072]{1,0:T(8,128)(2,1)} custom-call(s32[1]{0:T(128)S(6)} %copy.17.len_ref, s32[1]{0:T(128)S(6)} %copy.18.tsz_ref, bf16[8,3072]{1,0:T(8,128)(2,1)} %res_ref.1, bf16[1,16,1536]{2,1,0:T(8,128)(2,1)} %q_ref.1, bf16[1,16,256]{2,1,0:T(8,128)(2,1)} %tk_ref.1, bf16[1,16,256]{2,1,0:T(8,128)(2,1)} %tv_ref.1, s32[1,16,16]{2,1,0:T(8,128)} %mask_ref.1, ...), custom_call_target="tpu_custom_call" | custom-call | flops 4831838208 | bytes 37748736 | tf_op jit(solution)/shard_map/pallas_call | solution.py:499
  38.6 1.5 %fusion = (bf16[8,3072]{1,0:T(8,128)(2,1)}, bf16[8,3072]{1,0:T(8,128)(2,1)}) fusion(bf16[16,3072]{1,0:T(8,128)(2,1)} %shard_map.158), kind=kLoop, calls=%fused_computation | loop fusion | bytes 196608 | tf_op jit(solution)/shard_map/slice | solution.py:516
